TPU v7x, 256 devices: a whole 4x4x8 slice. The times are simulated.
256 devices in a mesh: inst: 8 (over y, core), rank: 32 (over x, z).
Axes of the slice: x: 4, y: 4, z: 8, core: 2. Of those that a mesh axis runs over, the one named last changes fastest.
Arguments:
- ffn_rows: bfloat16 [4096, 7168], P(('inst', 'rank')), parts along dimension 0, may hold values from -6 to 6
- row_counts: int32 [256], P('inst'), parts along dimension 0, may hold values from 1 to 16, as said below
- gate_weight: bfloat16 [7168, 9216], P(None, 'rank'), may hold values from -0.0625 to 0.0625
- up_weight: bfloat16 [7168, 9216], P(None, 'rank'), may hold values from -0.0625 to 0.0625
- down_weight: bfloat16 [9216, 7168], P('rank'), may hold values from -0.0625 to 0.0625
- queries: bfloat16 [1024, 64, 576], P(('inst', 'rank')), parts along dimension 0, may hold values from -20 to 20
- latent_cache: bfloat16 [1024, 64, 576], P(('inst', 'rank')), parts along dimension 0, may hold values from -6 to 6
- live_requests: int32 [256], P('inst'), parts along dimension 0, may hold values from 1 to 4, as said below
- cache_lengths: int32 [1024], P('inst'), parts along dimension 0, may hold values from 1 to 64, as said below
Outputs:
- ffn_out: bfloat16 [4096, 7168], P(('inst', 'rank')), parts along dimension 0
- attn_latent: bfloat16 [1024, 64, 512], P(('inst', 'rank')), parts along dimension 0
There are 8 independent parts, one for each index of `inst`. A program takes and returns all parts, laid end to end along the dimension named above; an argument that names none is the same for every part. Nothing has to cross between parts.
Inputs may be any that keep to these rules, and one draw needn't show every extreme that they name: `row_counts`: some rank has all its token slots live. `live_requests`: some rank has all its request slots live. `cache_lengths`: some slot is full.
All inputs are finite; a program needn't handle non-finite values.
Results may differ from a plain program's by a relative error of at most 0.011.
Values may be sent and summed in bfloat16 or wider, within the bound.
A program may use at most 128 MiB of HBM per device.

v0:
```python
import jax
import jax.numpy as jnp
from jax import lax
from jax.sharding import PartitionSpec as P

LATENT = 512


score_scale = 192.0 ** (-0.5)


def attend(query_rows, cache_rows, length):
    scores = (
        jnp.einsum("he,te->ht", query_rows, cache_rows, preferred_element_type=jnp.float32)
        * score_scale
    )
    positions = jnp.arange(cache_rows.shape[0])
    scores = jnp.where(positions[None, :] < length, scores, -1e30)
    peak = jnp.max(scores, axis=1, keepdims=True)
    expo = jnp.exp(scores - peak)
    probs = (expo / jnp.sum(expo, axis=1, keepdims=True)).astype(jnp.bfloat16)
    return jnp.dot(probs, cache_rows[:, :LATENT], preferred_element_type=jnp.float32).astype(
        jnp.bfloat16
    )


def attend_slots(query_block, cache_block, lengths, live_count):
    results = []
    for place in range(query_block.shape[0]):
        empty = jnp.zeros((query_block.shape[1], LATENT), jnp.bfloat16)
        results.append(
            lax.cond(
                place < live_count,
                lambda operands: attend(operands[0], operands[1], operands[2]),
                lambda operands: empty,
                (query_block[place], cache_block[place], lengths[place]),
            )
        )
    return jnp.stack(results)


def body(
    ffn_rows,
    row_counts,
    gate_weight,
    up_weight,
    down_weight,
    queries,
    latent_cache,
    live_requests,
    cache_lengths,
):
    position = lax.axis_index("rank")
    rows_dev = ffn_rows.shape[0]
    slots_dev = queries.shape[0]
    my_rows = lax.dynamic_slice_in_dim(row_counts, position, 1)[0]
    row_live = jnp.arange(rows_dev) < my_rows
    rows_in = jnp.where(row_live[:, None], ffn_rows, jnp.zeros_like(ffn_rows))
    block = lax.all_gather(rows_in, "rank", axis=0, tiled=True)
    gate = jnp.dot(block, gate_weight, preferred_element_type=jnp.float32)
    up_part = jnp.dot(block, up_weight, preferred_element_type=jnp.float32)
    terms = jnp.dot(
        (jax.nn.silu(gate) * up_part).astype(jnp.bfloat16),
        down_weight,
        preferred_element_type=jnp.float32,
    )
    ffn_out = lax.psum_scatter(terms, "rank", scatter_dimension=0, tiled=True).astype(jnp.bfloat16)
    my_lengths = lax.dynamic_slice_in_dim(cache_lengths, position * slots_dev, slots_dev)
    my_live = lax.dynamic_slice_in_dim(live_requests, position, 1)[0]
    attn_latent = attend_slots(queries, latent_cache, my_lengths, my_live)
    return (ffn_out, attn_latent)


def solution(mesh):
    placed = (
        P(("inst", "rank"), None),
        P("inst"),
        P(None, "rank"),
        P(None, "rank"),
        P("rank", None),
        P(("inst", "rank"), None, None),
        P(("inst", "rank"), None, None),
        P("inst"),
        P("inst"),
    )
    return jax.shard_map(
        body,
        mesh=mesh,
        in_specs=placed,
        out_specs=(P(("inst", "rank"), None), P(("inst", "rank"), None, None)),
        check_vma=False,
    )
```

profile of v0, /device:TPU:16, one launch (start us, length us, event | category | flops | bytes accessed | tf_op | source)
XLA Modules:
  0.0 371.0 jit_solution(4164079719884626112)
XLA Ops:
  7.2 0.0 all-gather.2.cloned.1.call-start
  7.2 1.2 dynamic_slice.9
  8.5 0.6 iota_compare_fusion.4
  9.1 1.7 broadcast_select_fusion
  10.9 0.0 reduce-scatter.2.cloned.1.call-start
  10.9 96.3 %all-gather.2.cloned.1.call-done = bf16[512,7168]{1,0:T(8,128)(2,1)} async-done(((bf16[16,7168]{1,0:T(8,128)(2,1)}), bf16[512,7168]{1,0:T(8,128)(2,1)}) %all-gather.2.cloned.1.call-update) | async-done | bytes 7340048 | tf_op jit(solution)/shard_map/all_gather | solution.py:59
  107.2 6.7 %fusion.37 = f32[512,288]{0,1:T(8,128)S(1)} fusion(bf16[512,7168]{1,0:T(8,128)(2,1)} %all-gather.2.cloned.1.call-done, bf16[7168,288]{0,1:T(8,128)(2,1)} %param.19), kind=kOutput, calls=%fused_computation.65 | convolution fusion | flops 2113929216 | bytes 12058624 | tf_op jit(solution)/shard_map/dot_general | solution.py:60
  114.0 0.8 copy-done.3
  114.8 2.3 fusion.32
  117.1 7.3 %fusion.38 = f32[512,7168]{1,0:T(8,128)} fusion(bf16[512,288]{0,1:T(8,128)(2,1)S(1)} %fusion.32, bf16[288,7168]{1,0:T(8,128)(2,1)S(1)} %copy-done), kind=kOutput, calls=%fused_computation.66 | convolution fusion | flops 2113929216 | bytes 19103744 | tf_op jit(solution)/shard_map/dot_general | solution.py:62
  124.5 0.6 copy-done.5
  125.1 0.6 dynamic_slice.10
  128.3 0.1 dynamic_slice.11
  128.4 1.7 conditional.5
  128.5 0.6 slice.48
  129.1 0.6 iota_compare_fusion.1
  129.7 0.2 fusion.34
  129.9 0.2 fusion.8
  130.1 0.5 conditional.4
  130.2 0.2 fusion.33
  130.4 0.2 fusion
  130.7 0.7 pad_maximum_fusion
  131.4 231.1 %reduce-scatter.2.cloned.1.call-done = f32[16,7168]{1,0:T(8,128)} async-done(((f32[512,7168]{1,0:T(8,128)}), f32[16,7168]{1,0:T(8,128)}) %reduce-scatter.2.cloned.1.call-update) | async-done | bytes 458768 | tf_op jit(solution)/shard_map/reduce_scatter | solution.py:67
  362.5 1.7 convert_element_type.55
  (23 shorter events, 0.2 us)
Async XLA Ops:
  7.2 100.1 %all-gather.2.cloned.1.call-start = ((), (), s32[]{:S(2)}) async-start(), calls=%async_computation.1 | async-start | bytes 7569408 | tf_op jit(solution)/shard_map/all_gather | solution.py:59
  10.9 351.6 %reduce-scatter.2.cloned.1.call-start = ((), (), s32[]{:S(2)}) async-start(), calls=%async_computation.2 | async-start | bytes 15138816 | tf_op jit(solution)/shard_map/reduce_scatter | solution.py:67
  107.2 6.7 %copy-start.2 = (bf16[512,7168]{1,0:T(8,128)(2,1)S(1)}, bf16[512,7168]{1,0:T(8,128)(2,1)}, u32[]{:S(2)}) copy-start(bf16[512,7168]{1,0:T(8,128)(2,1)} %all-gather.2.cloned.1.call-done) | copy-start | bytes 22020100
  107.2 7.5 %copy-start.3 = (bf16[7168,288]{0,1:T(8,128)(2,1)S(1)}, bf16[7168,288]{0,1:T(8,128)(2,1)}, u32[]{:S(2)}) copy-start(bf16[7168,288]{0,1:T(8,128)(2,1)} %param.20) | copy-start | bytes 12386308
  114.8 2.4 copy-start
  124.5 0.7 copy-start.5
  124.5 3.8 %copy-start.6 = (s32[128]{0:T(128)S(1)}, s32[128]{0:T(128)}, u32[]{:S(2)}) copy-start(s32[128]{0:T(128)} %param.25) | copy-start | bytes 1540
  124.5 3.9 %copy-start.1 = (bf16[4,64,576]{2,1,0:T(8,128)(2,1)S(1)}, bf16[4,64,576]{2,1,0:T(8,128)(2,1)}, u32[]{:S(2)}) copy-start(bf16[4,64,576]{2,1,0:T(8,128)(2,1)} %param.23) | copy-start | bytes 884740
  124.5 3.9 %copy-start.4 = (bf16[4,64,576]{2,1,0:T(8,128)(2,1)S(1)}, bf16[4,64,576]{2,1,0:T(8,128)(2,1)}, u32[]{:S(2)}) copy-start(bf16[4,64,576]{2,1,0:T(8,128)(2,1)} %param.22) | copy-start | bytes 884740
Sparse Core Ops, SparseCore 0:
  11.1 96.0 all-gather.1
  124.6 237.7 reduce-scatter.1
where the time goes:
time: 371 us
  waiting for transfers between devices  327 us (88%)
  matrix products  17.2 us (5%)
  between operations  16.7 us (5%)
  other arithmetic  5.6 us (2%)
  local copies, waits for them, and re-layouts  3.92 us (1%)
    reduce_scatter x1, waiting for transfers between devices, body(): lax.psum_scatter(terms, 'rank', scatter_dimension=0, tiled=True)  231 us
    all_gather x1, waiting for transfers between devices, body(): block = lax.all_gather(rows_in, 'rank', axis=0, tiled=True)  96.3 us
  transfers between devices with their start and end apart: 2, of which 2 were waited for; matrix products, arithmetic and copies ran while one was open for 1% of the time, Pallas kernels for 0%

commit v1 on v0

v1 whole, which is shorter than its diff:
```python
import functools

import jax
import jax.numpy as jnp
from jax import lax
from jax.experimental import pallas as pl
from jax.experimental.pallas import tpu as pltpu
from jax.sharding import PartitionSpec as P

MESH = pl.DeviceIdType.MESH
D, FF, ROWS, LATENT = 7168, 288, 16, 512
NX, NZ, NY = 4, 8, 4
GROUP = NX * ROWS
SLICE = D // NX
HALF = SLICE // 2
TILE = 128
CA = 26 * TILE
A0 = 13 * TILE
CB = D - CA
B0 = 15 * TILE
KCH = 1024
score_scale = 192.0 ** (-0.5)


def layout():
    names = {}

    def add(name, count):
        names[name] = len_box[0]
        len_box[0] += count

    len_box = [0]
    add("a1", 3)
    add("b1", 8)
    add("a2", 32)
    add("b2", 32)
    add("w1", 3)
    add("w2", 9)
    add("wc", 12)
    add("h", 24)
    add("r", 14)
    add("f", 6)
    return names, len_box[0]


SEM, NSEM = layout()


def kernel(
    counts, live, lengths, rows_in, wg_in, wu_in, wd_in, q_in, c_in, ffn_out, attn_out,
    xi, xb, wg, wu, wd, qb, cb, acc, hid, part, sbuf, rbuf, fs, fo, ssem, rsem, lsem,
):
    inst = lax.axis_index("inst")
    rank = lax.axis_index("rank")
    y, c = inst // 2, inst % 2
    x, z = rank // NZ, rank % NZ
    yhi, ylo = y // 2, y % 2

    def at_x(k):
        return (inst, ((x + NX + k) % NX) * NZ + z)

    def at_z(k):
        return (inst, x * NZ + (z + NZ + k) % NZ)

    def at_y(k):
        return (((y + NY + k) % NY) * 2 + c, rank)

    other = (y * 2 + (1 - c), rank)
    zp, zm, xp, xm = at_z(1), at_z(-1), at_x(1), at_x(-1)

    loads = [
        pltpu.make_async_copy(rows_in, xi, lsem.at[0]),
        pltpu.make_async_copy(q_in, qb, lsem.at[1]),
        pltpu.make_async_copy(c_in, cb, lsem.at[2]),
        pltpu.make_async_copy(wg_in, wg, lsem.at[3]),
        pltpu.make_async_copy(wu_in, wu, lsem.at[4]),
        pltpu.make_async_copy(
            wd_in.at[:, pl.ds(pl.multiple_of(x * SLICE, TILE), SLICE)],
            wd.at[pl.ds(pl.multiple_of(x * FF, 16), FF), :],
            lsem.at[5],
        ),
    ]
    loads[0].start()

    barrier = pltpu.get_barrier_semaphore()
    peers = [zp, zm, xp, xm, at_x(2), at_y(1), at_y(-1), at_y(2), other]
    for peer in peers:
        pl.semaphore_signal(barrier, inc=1, device_id=peer, device_id_type=MESH)
    for load in loads[1:]:
        load.start()
    loads[0].wait()
    mine = pl.ds(pl.multiple_of((z * NX + x) * ROWS, ROWS), ROWS)
    row_live = lax.broadcasted_iota(jnp.int32, (ROWS, 1), 0) < counts[rank]
    xb[mine, :] = jnp.where(row_live, xi[...], jnp.zeros_like(xi[...]))
    pl.semaphore_wait(barrier, len(peers))

    sent = []

    def send(src, dst, index, peer):
        copy = pltpu.make_async_remote_copy(
            src, dst, ssem.at[index], rsem.at[index], device_id=peer, device_id_type=MESH
        )
        copy.start()
        sent.append(copy)

    def recv(dst, index):
        pltpu.make_async_remote_copy(
            dst, dst, ssem.at[index], rsem.at[index], device_id=zp, device_id_type=MESH
        ).wait_recv()

    def block(dx, dz):
        at = ((z + NZ + dz) % NZ) * NX + (x + NX + dx) % NX
        return pl.ds(pl.multiple_of(at * ROWS, ROWS), ROWS)

    def group(dz):
        return pl.ds(pl.multiple_of(((z + NZ + dz) % NZ) * GROUP, GROUP), GROUP)

    full_a, half_a = pl.ds(0, CA), (pl.ds(0, A0), pl.ds(A0, CA - A0))
    full_b, half_b = pl.ds(CA, CB), (pl.ds(CA, B0), pl.ds(CA + B0, CB - B0))
    toward = (zp, zm)

    def a2_index(way, hop, j):
        return SEM["a2"] + (way * 4 + hop - 1) * 4 + j

    def b1_index(way, hop):
        return SEM["b1"] + way * 4 + hop - 1

    def a2_send(way, hop, j):
        sign = -1 if way == 0 else 1
        cols = full_a if hop < 4 else half_a[way]
        ref = xb.at[block(-j, sign * (hop - 1)), cols]
        send(ref, ref, a2_index(way, hop, j), toward[way])

    def a2_recv(way, hop, j):
        sign = -1 if way == 0 else 1
        cols = full_a if hop < 4 else half_a[way]
        recv(xb.at[block(-j, sign * hop), cols], a2_index(way, hop, j))

    def b1_send(way, hop):
        sign = -1 if way == 0 else 1
        cols = full_b if hop < 4 else half_b[way]
        ref = xb.at[block(0, sign * (hop - 1)), cols]
        send(ref, ref, b1_index(way, hop), toward[way])

    def b1_recv(way, hop):
        sign = -1 if way == 0 else 1
        cols = full_b if hop < 4 else half_b[way]
        recv(xb.at[block(0, sign * hop), cols], b1_index(way, hop))

    def b2_index(dz, kind):
        return SEM["b2"] + (dz % NZ) * 4 + kind

    def b2_send(dz):
        ref = xb.at[block(0, dz), full_b]
        send(ref, ref, b2_index(dz, 0), xp)
        send(ref, ref, b2_index(dz, 1), xm)

    def b2_pass(dz):
        recv(xb.at[block(-1, dz), full_b], b2_index(dz, 0))
        ref = xb.at[block(-1, dz), half_b[0]]
        send(ref, ref, b2_index(dz, 2), xp)
        recv(xb.at[block(1, dz), full_b], b2_index(dz, 1))
        ref = xb.at[block(1, dz), half_b[1]]
        send(ref, ref, b2_index(dz, 3), xm)

    def b2_last(dz):
        recv(xb.at[block(-2, dz), half_b[0]], b2_index(dz, 2))
        recv(xb.at[block(2, dz), half_b[1]], b2_index(dz, 3))

    def wd_piece(xs, yy, start, count):
        row = xs * FF + (yy // 2) * 144 + start
        col = (yy % 2) * HALF
        return wd.at[pl.ds(pl.multiple_of(row, 16), count), pl.ds(pl.multiple_of(col, TILE), HALF)]

    def w1_send(k):
        to = (x + k) % NX
        src = wd_in.at[
            pl.ds(pl.multiple_of(yhi * 144 + c * 64, 16), 80),
            pl.ds(pl.multiple_of(to * SLICE + ylo * HALF, TILE), HALF),
        ]
        send(src, wd_piece(x, y, c * 64, 80), SEM["w1"] + k - 1, at_x(k))

    def wc_send(k, m):
        ref = wd_piece((x + NX - k) % NX, (y + NY - m) % NY, c * 80, 64)
        send(ref, ref, SEM["wc"] + (k - 1) * 4 + m, other)

    def w1_pass(k):
        ref = wd_piece((x + NX - k) % NX, y, c * 64, 80)
        recv(ref, SEM["w1"] + k - 1)
        for m in (1, 3, 2):
            send(ref, ref, SEM["w2"] + (k - 1) * 3 + m - 1, at_y(m))
        wc_send(k, 0)

    def w2_pass(k, m):
        ref = wd_piece((x + NX - k) % NX, (y + NY - m) % NY, c * 64, 80)
        recv(ref, SEM["w2"] + (k - 1) * 3 + m - 1)
        wc_send(k, m)

    def wc_recv(k, m):
        ref = wd_piece((x + NX - k) % NX, (y + NY - m) % NY, (1 - c) * 80, 64)
        recv(ref, SEM["wc"] + (k - 1) * 4 + m)

    pieces = []

    def tick(count=1):
        for _ in range(count):
            if pieces:
                pieces.pop(0)()

    def drain():
        while pieces:
            pieces.pop(0)()

    def attend(slot):
        keys = cb[slot]
        scores = lax.dot_general(
            qb[slot], keys, (((1,), (1,)), ((), ())), preferred_element_type=jnp.float32
        ) * score_scale
        places = lax.broadcasted_iota(jnp.int32, scores.shape, 1)
        scores = jnp.where(places < lengths[rank * 4 + slot], scores, -1e30)
        expo = jnp.exp(scores - jnp.max(scores, axis=1, keepdims=True))
        probs = (expo / jnp.sum(expo, axis=1, keepdims=True)).astype(jnp.bfloat16)
        value = jnp.dot(probs, keys[:, :LATENT], preferred_element_type=jnp.float32)
        keep = jnp.full((1, 1), slot, jnp.int32) < live[rank]
        attn_out[slot] = jnp.where(keep, value, 0.0).astype(jnp.bfloat16)

    def up_piece(pair, k):
        cols = pl.ds(k * KCH, KCH)
        rows = jnp.concatenate([xb[group(dz), cols] for dz in pair], axis=0)
        for which, weight in enumerate((wg, wu)):
            term = jnp.dot(rows, weight[cols, :], preferred_element_type=jnp.float32)
            if k == 0:
                acc[which] = term
            else:
                acc[which] += term

    def h_index(dz, k):
        return SEM["h"] + (dz % NZ) * 3 + k - 1

    def hidden_piece(pair):
        gate, up = acc[0], acc[1]
        value = (gate / (1.0 + jnp.exp(-gate)) * up).astype(jnp.bfloat16)
        for i, dz in enumerate(pair):
            hid[x, group(dz), :] = value[i * GROUP:(i + 1) * GROUP]
        for dz in pair:
            ref = hid.at[x, group(dz), :]
            for k in (1, 3, 2):
                send(ref, ref, h_index(dz, k), at_x(k))

    def hidden_wait(pair):
        for dz in pair:
            for k in (1, 3, 2):
                recv(hid.at[(x + NX - k) % NX, group(dz), :], h_index(dz, k))

    def down_piece(pair, n):
        cols = pl.ds(n * 256, 256)
        total = None
        for xs in range(NX):
            rows = jnp.concatenate([hid[xs, group(dz), :] for dz in pair], axis=0)
            term = jnp.dot(
                rows, wd[xs * FF:(xs + 1) * FF, cols], preferred_element_type=jnp.float32
            )
            total = term if total is None else total + term
        for i, dz in enumerate(pair):
            part[group(dz), cols] = total[i * GROUP:(i + 1) * GROUP]

    def queue_up(pair):
        for k in range(D // KCH):
            pieces.append(functools.partial(up_piece, pair, k))
        pieces.append(functools.partial(hidden_piece, pair))

    def queue_down(pair):
        pieces.append(functools.partial(hidden_wait, pair))
        for n in range(SLICE // 256):
            pieces.append(functools.partial(down_piece, pair, n))

    half_cols = (pl.ds(0, HALF), pl.ds(HALF, HALF))

    def ring_step(step):
        for way in range(2):
            sign = -1 if way == 0 else 1
            value = part[group(sign * (1 + step)), half_cols[way]]
            if step > 0:
                recv(rbuf.at[way, step - 1], SEM["r"] + way * 7 + step - 1)
                value = value + rbuf[way, step - 1].astype(jnp.float32)
            sbuf[way, step] = value.astype(jnp.bfloat16)
            send(sbuf.at[way, step], rbuf.at[way, step], SEM["r"] + way * 7 + step, toward[way])

    for k in (1, 3, 2):
        ref = xb.at[mine, full_a]
        send(ref, ref, SEM["a1"] + k - 1, at_x(k))
    for way in range(2):
        b1_send(way, 1)
        a2_send(way, 1, 0)
    b2_send(0)
    for k in (1, 3, 2):
        w1_send(k)
    loads[1].wait()
    loads[2].wait()
    attend(0)
    for k in (1, 3, 2):
        recv(xb.at[block(-k, 0), full_a], SEM["a1"] + k - 1)
        for way in range(2):
            a2_send(way, 1, k)
    b2_pass(0)
    attend(1)
    for k in (1, 3, 2):
        w1_pass(k)

    pieces.append(functools.partial(attend, 2))
    pieces.append(functools.partial(attend, 3))

    for hop in (1, 2, 3):
        for way in range(2):
            sign = -1 if way == 0 else 1
            b1_recv(way, hop)
            b1_send(way, hop + 1)
            if hop < 4:
                b2_send(sign * hop)
            tick()
        for j in (0, 1, 3, 2):
            for way in range(2):
                a2_recv(way, hop, j)
                a2_send(way, hop + 1, j)
            tick()
            if hop == 1 and j != 0:
                for m in (1, 3, 2):
                    w2_pass(j, m)
        for way in range(2):
            sign = -1 if way == 0 else 1
            b2_pass(sign * hop)
            tick()
        if hop == 1:
            b2_last(0)
            loads[3].wait()
            loads[4].wait()
            loads[5].wait()
            for k in (1, 2, 3):
                for m in range(4):
                    wc_recv(k, m)
        for way in range(2):
            b2_last((-1 if way == 0 else 1) * hop)
        drain()
        queue_up((-hop, hop))
        if hop > 1:
            queue_down((1 - hop, hop - 1))

    for way in range(2):
        b1_recv(way, 4)
    b2_send(4)
    tick(4)
    for j in (0, 1, 3, 2):
        for way in range(2):
            a2_recv(way, 4, j)
        tick()
    b2_pass(4)
    tick(4)
    b2_last(4)
    drain()
    ring_step(0)
    queue_up((0, 4))
    drain()
    queue_down((-3, 3))
    drain()
    ring_step(1)
    queue_down((0, 4))
    drain()
    for step in range(2, 7):
        ring_step(step)

    for way in range(2):
        recv(rbuf.at[way, 6], SEM["r"] + way * 7 + 6)
        value = part[group(0), half_cols[way]] + rbuf[way, 6].astype(jnp.float32)
        fs[way] = value.astype(jnp.bfloat16)
        cols = pl.ds(pl.multiple_of(x * SLICE + way * HALF, TILE), HALF)
        for k in (1, 3, 2):
            to = (x + k) % NX
            send(
                fs.at[way, pl.ds(pl.multiple_of(to * ROWS, ROWS), ROWS), :],
                fo.at[:, cols], SEM["f"] + way * 3 + k - 1, at_x(k),
            )
        fo[:, cols] = fs[way, pl.ds(pl.multiple_of(x * ROWS, ROWS), ROWS), :]
    for copy in sent:
        copy.wait_send()
    for way in range(2):
        for k in (1, 3, 2):
            cols = pl.ds(pl.multiple_of(((x + NX - k) % NX) * SLICE + way * HALF, TILE), HALF)
            recv(fo.at[:, cols], SEM["f"] + way * 3 + k - 1)
    ffn_out[...] = fo[...]


def body(rows, counts, gate, up, down, queries, cache, live, lengths):
    bf16, f32 = jnp.bfloat16, jnp.float32
    smem = pl.BlockSpec(memory_space=pltpu.SMEM)
    hbm = pl.BlockSpec(memory_space=pl.ANY)
    vmem = pl.BlockSpec(memory_space=pltpu.VMEM)
    return pl.pallas_call(
        kernel,
        out_shape=(
            jax.ShapeDtypeStruct((ROWS, D), bf16),
            jax.ShapeDtypeStruct((4, 64, LATENT), bf16),
        ),
        in_specs=[smem] * 3 + [hbm] * 6,
        out_specs=(vmem, vmem),
        scratch_shapes=[
            pltpu.VMEM((ROWS, D), bf16),
            pltpu.VMEM((NZ * GROUP, D), bf16),
            pltpu.VMEM((D, FF), bf16),
            pltpu.VMEM((D, FF), bf16),
            pltpu.VMEM((NX * FF, SLICE), bf16),
            pltpu.VMEM((4, 64, 576), bf16),
            pltpu.VMEM((4, 64, 576), bf16),
            pltpu.VMEM((2, 2 * GROUP, FF), f32),
            pltpu.VMEM((NX, NZ * GROUP, FF), bf16),
            pltpu.VMEM((NZ * GROUP, SLICE), f32),
            pltpu.VMEM((2, 7, GROUP, HALF), bf16),
            pltpu.VMEM((2, 7, GROUP, HALF), bf16),
            pltpu.VMEM((2, GROUP, HALF), bf16),
            pltpu.VMEM((ROWS, D), bf16),
            pltpu.SemaphoreType.DMA((NSEM,)),
            pltpu.SemaphoreType.DMA((NSEM,)),
            pltpu.SemaphoreType.DMA((6,)),
        ],
        compiler_params=pltpu.CompilerParams(
            collective_id=1, has_side_effects=True, vmem_limit_bytes=56 * 2**20
        ),
        cost_estimate=pl.CostEstimate(
            flops=2 * 512 * D * FF * 3, bytes_accessed=16 * 2**20, transcendentals=512 * FF
        ),
    )(counts, live, lengths, rows, gate, up, down, queries, cache)


def solution(mesh):
    placed = (
        P(("inst", "rank"), None),
        P("inst"),
        P(None, "rank"),
        P(None, "rank"),
        P("rank", None),
        P(("inst", "rank"), None, None),
        P(("inst", "rank"), None, None),
        P("inst"),
        P("inst"),
    )
    return jax.shard_map(
        body,
        mesh=mesh,
        in_specs=placed,
        out_specs=(P(("inst", "rank"), None), P(("inst", "rank"), None, None)),
        check_vma=False,
    )
```

time: 371 us -> 140 us (0.38)
  waiting for transfers between devices: 327 us -> 0 us
  Pallas kernels: 0 us -> 120 us
  matrix products: 17.2 us -> 0 us
  between operations: 16.7 us -> 0.64 us
  local copies, waits for them, and re-layouts: 3.92 us -> 18.1 us
  other arithmetic: 5.6 us -> 0 us
    reduce_scatter x1 -> x0, waiting for transfers between devices: 231 us -> none  [body(): lax.psum_scatter(terms, 'rank', scatter_dimension=0, tiled=True)]
    pallas_call x0 -> x1, Pallas kernels: none -> 120 us  [body(): pl.pallas_call(kernel, out_shape=(jax.ShapeDtypeStruct((ROWS, D), bf16),...]
    all_gather x1 -> x0, waiting for transfers between devices: 96.3 us -> none  [body(): block = lax.all_gather(rows_in, 'rank', axis=0, tiled=True)]
    dot_general x7 -> x0, matrix products: 17.2 us -> none  [the longest x1 7.33 us: body(): jnp.dot((jax.nn.silu(gate) * up_part).astype(jnp.bfloat16), down_weight,...]
    unnamed x14 -> x4, local copies, waits for them, and re-layouts: 1.41 us -> 18.1 us
  transfers between devices with their start and end apart: 2 -> 0, of which waited for: 2 -> 0; matrix products, arithmetic and copies ran while one was open for 1% -> 0% of each run, Pallas kernels for 0% -> 0%
where the time goes in v1:
time: 140 us; the launch traced here: 138 us
  Pallas kernels  120 us (86%)
  local copies, waits for them, and re-layouts  18.1 us (13%)
    pallas_call x1, Pallas kernels, body(): pl.pallas_call(kernel, out_shape=(jax.ShapeDtypeStruct((ROWS, D), bf16),...  120 us
    unnamed x4, local copies, waits for them, and re-layouts  18.1 us

profile of v1, /device:TPU:16, one launch (start us, length us, event | category | flops | bytes accessed | tf_op | source)
XLA Modules:
  0.0 138.5 jit_solution(5474028873081356244)
XLA Ops:
  0.6 7.4 %copy.11.wg_in = bf16[7168,288]{1,0:T(8,128)(2,1)} copy(bf16[7168,288]{0,1:T(8,128)(2,1)} %param.11) | data formatting | bytes 8257536 | tf_op args[2]
  8.0 7.4 %copy.12.wu_in = bf16[7168,288]{1,0:T(8,128)(2,1)} copy(bf16[7168,288]{0,1:T(8,128)(2,1)} %param.12) | data formatting | bytes 8257536 | tf_op args[3]
  15.4 119.8 %shard_map.104 = (bf16[16,7168]{1,0:T(8,128)(2,1)}, bf16[4,64,512]{2,1,0:T(8,128)(2,1)}) custom-call(s32[32]{0:T(128)} %counts.1, s32[32]{0:T(128)} %live.1, s32[128]{0:T(128)} %lengths.1, bf16[16,7168]{1,0:T(8,128)(2,1)} %rows_in.1, bf16[7168,288]{1,0:T(8,128)(2,1)} %copy.11.wg_in, bf16[7168,288]{1,0:T(8,128)(2,1)} %copy.12.wu_in, bf16[288,7168]{1,0:T(8,128)(2,1)} %wd_in.1, ...), custom_call_target="tpu_custom_call" | custom-call | flops 6341787648 | bytes 16777216 | tf_op jit(solution)/shard_map/pallas_call | solution.py:397
  135.2 1.6 %copy.15 = bf16[16,7168]{1,0:T(8,128)(2,1)} copy(bf16[16,7168]{1,0:T(8,128)(2,1)} %get-tuple-element.4) | data formatting | bytes 458752
  136.8 1.7 %copy.16 = bf16[4,64,512]{2,1,0:T(8,128)(2,1)} copy(bf16[4,64,512]{2,1,0:T(8,128)(2,1)} %get-tuple-element.5) | data formatting | bytes 524288

commit v2 on v1

--- a/solution.py
+++ b/solution.py
@@ -14,11 +14,12 @@
 SLICE = D // NX
 HALF = SLICE // 2
 TILE = 128
-CA = 26 * TILE
-A0 = 13 * TILE
+CA = 30 * TILE
+A0 = 15 * TILE
 CB = D - CA
-B0 = 15 * TILE
+B0 = 13 * TILE
 KCH = 1024
+SUBS, SUB = 4, 16
 score_scale = 192.0 ** (-0.5)
 
 
@@ -38,7 +39,8 @@
     add("w2", 9)
     add("wc", 12)
     add("h", 24)
-    add("r", 14)
+    add("ht", 24)
+    add("r", 56)
     add("f", 6)
     return names, len_box[0]
 
@@ -48,7 +50,7 @@
 
 def kernel(
     counts, live, lengths, rows_in, wg_in, wu_in, wd_in, q_in, c_in, ffn_out, attn_out,
-    xi, xb, wg, wu, wd, qb, cb, acc, hid, part, sbuf, rbuf, fs, fo, ssem, rsem, lsem,
+    xi, xb, wgu, wd, qb, cb, acc, hid, tail, rest, part, sbuf, rbuf, fs, fo, ssem, rsem, lsem,
 ):
     inst = lax.axis_index("inst")
     rank = lax.axis_index("rank")
@@ -72,8 +74,8 @@
         pltpu.make_async_copy(rows_in, xi, lsem.at[0]),
         pltpu.make_async_copy(q_in, qb, lsem.at[1]),
         pltpu.make_async_copy(c_in, cb, lsem.at[2]),
-        pltpu.make_async_copy(wg_in, wg, lsem.at[3]),
-        pltpu.make_async_copy(wu_in, wu, lsem.at[4]),
+        pltpu.make_async_copy(wg_in, wgu.at[0:FF, :], lsem.at[3]),
+        pltpu.make_async_copy(wu_in, wgu.at[FF:2 * FF, :], lsem.at[4]),
         pltpu.make_async_copy(
             wd_in.at[:, pl.ds(pl.multiple_of(x * SLICE, TILE), SLICE)],
             wd.at[pl.ds(pl.multiple_of(x * FF, 16), FF), :],
@@ -227,40 +229,69 @@
     def up_piece(pair, k):
         cols = pl.ds(k * KCH, KCH)
         rows = jnp.concatenate([xb[group(dz), cols] for dz in pair], axis=0)
-        for which, weight in enumerate((wg, wu)):
-            term = jnp.dot(rows, weight[cols, :], preferred_element_type=jnp.float32)
+        for which in range(2):
+            term = lax.dot_general(
+                rows, wgu[which * FF:(which + 1) * FF, cols], (((1,), (1,)), ((), ())),
+                preferred_element_type=jnp.float32,
+            )
+            size = len(pair) * GROUP
             if k == 0:
-                acc[which] = term
+                acc[which, :size] = term
             else:
-                acc[which] += term
-
-    def h_index(dz, k):
-        return SEM["h"] + (dz % NZ) * 3 + k - 1
+                acc[which, :size] += term
+
+    def h_send(dz, part_of):
+        for k in (1, 3, 2):
+            at = ((dz % NZ) * 3 + k - 1)
+            if part_of == 0:
+                ref = hid.at[x, group(dz), :]
+                send(ref, ref, SEM["h"] + at, at_x(k))
+            else:
+                ref = tail.at[x, quarter(dz), :]
+                send(ref, ref, SEM["ht"] + at, at_x(k))
+
+    def quarter(dz):
+        return pl.ds(pl.multiple_of(((z + NZ + dz) % NZ) * ROWS, ROWS), ROWS)
 
     def hidden_piece(pair):
-        gate, up = acc[0], acc[1]
+        size = len(pair) * GROUP
+        gate, up = acc[0, :size], acc[1, :size]
         value = (gate / (1.0 + jnp.exp(-gate)) * up).astype(jnp.bfloat16)
         for i, dz in enumerate(pair):
-            hid[x, group(dz), :] = value[i * GROUP:(i + 1) * GROUP]
-        for dz in pair:
-            ref = hid.at[x, group(dz), :]
-            for k in (1, 3, 2):
-                send(ref, ref, h_index(dz, k), at_x(k))
+            rows = value[i * GROUP:(i + 1) * GROUP]
+            hid[x, group(dz), :] = rows[:, :256]
+            tail[x, quarter(dz), :] = jnp.concatenate(
+                [rows[n * ROWS:(n + 1) * ROWS, 256:] for n in range(4)], axis=1
+            )
+            h_send(dz, 0)
+            h_send(dz, 1)
 
     def hidden_wait(pair):
         for dz in pair:
             for k in (1, 3, 2):
-                recv(hid.at[(x + NX - k) % NX, group(dz), :], h_index(dz, k))
+                at = ((dz % NZ) * 3 + k - 1)
+                recv(hid.at[(x + NX - k) % NX, group(dz), :], SEM["h"] + at)
+                recv(tail.at[(x + NX - k) % NX, quarter(dz), :], SEM["ht"] + at)
+        for i, dz in enumerate(pair):
+            packed = [tail[xs, quarter(dz), :] for xs in range(NX)]
+            rest[i * GROUP:(i + 1) * GROUP, :] = jnp.concatenate(
+                [
+                    jnp.concatenate([p[:, n * 32:(n + 1) * 32] for p in packed], axis=1)
+                    for n in range(4)
+                ],
+                axis=0,
+            )
 
     def down_piece(pair, n):
         cols = pl.ds(n * 256, 256)
-        total = None
+        size = len(pair) * GROUP
+        lower = jnp.concatenate([wd[xs * FF + 256:(xs + 1) * FF, cols] for xs in range(NX)], axis=0)
+        total = jnp.dot(rest[:size, :], lower, preferred_element_type=jnp.float32)
         for xs in range(NX):
             rows = jnp.concatenate([hid[xs, group(dz), :] for dz in pair], axis=0)
-            term = jnp.dot(
-                rows, wd[xs * FF:(xs + 1) * FF, cols], preferred_element_type=jnp.float32
+            total += jnp.dot(
+                rows, wd[xs * FF:xs * FF + 256, cols], preferred_element_type=jnp.float32
             )
-            total = term if total is None else total + term
         for i, dz in enumerate(pair):
             part[group(dz), cols] = total[i * GROUP:(i + 1) * GROUP]
 
@@ -277,99 +308,146 @@
     half_cols = (pl.ds(0, HALF), pl.ds(HALF, HALF))
 
     def ring_step(step):
+        for sub in range(SUBS):
+            rows = pl.ds(sub * SUB, SUB)
+            for way in range(2):
+                index = SEM["r"] + (way * 7 + step) * SUBS + sub
+                dz = (-1 if way == 0 else 1) * (1 + step)
+                at = ((z + NZ + dz) % NZ) * GROUP + sub * SUB
+                value = part[pl.ds(pl.multiple_of(at, SUB), SUB), half_cols[way]]
+                if step > 0:
+                    recv(rbuf.at[way, step - 1, rows], index - SUBS)
+                    value = value + rbuf[way, step - 1, rows].astype(jnp.float32)
+                sbuf[way, step, rows] = value.astype(jnp.bfloat16)
+                send(sbuf.at[way, step, rows], rbuf.at[way, step, rows], index, toward[way])
+
+    ways = ((0, -1), (1, 1))
+
+    def b1(hop):
+        for way, sign in ways:
+            b1_recv(way, hop)
+            if hop < 4:
+                b1_send(way, hop + 1)
+                b2_send(sign * hop)
+        if hop == 4:
+            b2_send(4)
+
+    def a2(hop, j):
+        for way, sign in ways:
+            a2_recv(way, hop, j)
+            if hop < 4:
+                a2_send(way, hop + 1, j)
+
+    def last(hop):
+        for way, sign in ways[:1 if hop in (0, 4) else 2]:
+            b2_last(sign * hop)
+
+    def a1(k):
+        recv(xb.at[block(-k, 0), full_a], SEM["a1"] + k - 1)
         for way in range(2):
-            sign = -1 if way == 0 else 1
-            value = part[group(sign * (1 + step)), half_cols[way]]
-            if step > 0:
-                recv(rbuf.at[way, step - 1], SEM["r"] + way * 7 + step - 1)
-                value = value + rbuf[way, step - 1].astype(jnp.float32)
-            sbuf[way, step] = value.astype(jnp.bfloat16)
-            send(sbuf.at[way, step], rbuf.at[way, step], SEM["r"] + way * 7 + step, toward[way])
+            a2_send(way, 1, k)
 
     for k in (1, 3, 2):
         ref = xb.at[mine, full_a]
         send(ref, ref, SEM["a1"] + k - 1, at_x(k))
-    for way in range(2):
+    for way, sign in ways:
         b1_send(way, 1)
         a2_send(way, 1, 0)
     b2_send(0)
-    for k in (1, 3, 2):
-        w1_send(k)
     loads[1].wait()
     loads[2].wait()
     attend(0)
+    a1(1)
+    a1(3)
+    b1(1)
+    a1(2)
     for k in (1, 3, 2):
-        recv(xb.at[block(-k, 0), full_a], SEM["a1"] + k - 1)
-        for way in range(2):
-            a2_send(way, 1, k)
+        w1_send(k)
+    a2(1, 0)
     b2_pass(0)
     attend(1)
-    for k in (1, 3, 2):
-        w1_pass(k)
-
-    pieces.append(functools.partial(attend, 2))
-    pieces.append(functools.partial(attend, 3))
-
-    for hop in (1, 2, 3):
-        for way in range(2):
-            sign = -1 if way == 0 else 1
-            b1_recv(way, hop)
-            b1_send(way, hop + 1)
-            if hop < 4:
-                b2_send(sign * hop)
-            tick()
-        for j in (0, 1, 3, 2):
-            for way in range(2):
-                a2_recv(way, hop, j)
-                a2_send(way, hop + 1, j)
-            tick()
-            if hop == 1 and j != 0:
-                for m in (1, 3, 2):
-                    w2_pass(j, m)
-        for way in range(2):
-            sign = -1 if way == 0 else 1
-            b2_pass(sign * hop)
-            tick()
-        if hop == 1:
-            b2_last(0)
-            loads[3].wait()
-            loads[4].wait()
-            loads[5].wait()
-            for k in (1, 2, 3):
-                for m in range(4):
-                    wc_recv(k, m)
-        for way in range(2):
-            b2_last((-1 if way == 0 else 1) * hop)
-        drain()
-        queue_up((-hop, hop))
-        if hop > 1:
-            queue_down((1 - hop, hop - 1))
+    a2(1, 1)
+    attend(2)
+    a2(1, 3)
+    b2_pass(-1)
+    attend(3)
+    a2(1, 2)
+    b2_pass(1)
+    for load in loads[3:]:
+        load.wait()
+
+    b1(2)
+    a2(2, 0)
+    last(0)
+    a2(2, 1)
+    last(1)
+    queue_up((-1, 0, 1))
+    tick(2)
+    w1_pass(1)
+    a2(2, 3)
+    tick(2)
+    b2_pass(-2)
+    w1_pass(3)
+    a2(2, 2)
+    tick(2)
+    b2_pass(2)
+    w1_pass(2)
+    b1(3)
+    drain()
+    a2(3, 0)
+    a2(3, 1)
+    last(2)
+    queue_up((-2, 2))
+    tick(2)
+    for m in (1, 3, 2):
+        w2_pass(1, m)
+    a2(3, 3)
+    tick(2)
+    b2_pass(-3)
+    for m in (1, 3, 2):
+        w2_pass(3, m)
+    a2(3, 2)
+    tick(2)
+    b2_pass(3)
+    for m in (1, 3, 2):
+        w2_pass(2, m)
+    drain()
+    b1(4)
+    for k in (1, 2, 3):
+        for m in range(4):
+            wc_recv(k, m)
+    queue_down((-1, 0, 1))
+    drain()
+    ring_step(0)
+    a2(4, 0)
+    last(3)
+    queue_up((-3, 3))
+    tick(4)
+    a2(4, 1)
+    b2_pass(4)
+    drain()
+    queue_down((-2, 2))
+    drain()
+    ring_step(1)
+    a2(4, 3)
+    a2(4, 2)
+    for k in range(3):
+        up_piece((4,), k)
+    last(4)
+    for k in range(3, D // KCH):
+        up_piece((4,), k)
+    hidden_piece((4,))
+    queue_down((-3, 3))
+    drain()
+    ring_step(2)
+    queue_down((4,))
+    drain()
+    for step in range(3, 7):
+        ring_step(step)
 
     for way in range(2):
-        b1_recv(way, 4)
-    b2_send(4)
-    tick(4)
-    for j in (0, 1, 3, 2):
-        for way in range(2):
-            a2_recv(way, 4, j)
-        tick()
-    b2_pass(4)
-    tick(4)
-    b2_last(4)
-    drain()
-    ring_step(0)
-    queue_up((0, 4))
-    drain()
-    queue_down((-3, 3))
-    drain()
-    ring_step(1)
-    queue_down((0, 4))
-    drain()
-    for step in range(2, 7):
-        ring_step(step)
-
-    for way in range(2):
-        recv(rbuf.at[way, 6], SEM["r"] + way * 7 + 6)
+        for sub in range(SUBS):
+            recv(rbuf.at[way, 6, pl.ds(sub * SUB, SUB)], SEM["r"] + (way * 7 + 6) * SUBS + sub)
         value = part[group(0), half_cols[way]] + rbuf[way, 6].astype(jnp.float32)
         fs[way] = value.astype(jnp.bfloat16)
         cols = pl.ds(pl.multiple_of(x * SLICE + way * HALF, TILE), HALF)
@@ -405,13 +483,14 @@
         scratch_shapes=[
             pltpu.VMEM((ROWS, D), bf16),
             pltpu.VMEM((NZ * GROUP, D), bf16),
-            pltpu.VMEM((D, FF), bf16),
-            pltpu.VMEM((D, FF), bf16),
+            pltpu.VMEM((2 * FF, D), bf16),
             pltpu.VMEM((NX * FF, SLICE), bf16),
             pltpu.VMEM((4, 64, 576), bf16),
             pltpu.VMEM((4, 64, 576), bf16),
-            pltpu.VMEM((2, 2 * GROUP, FF), f32),
-            pltpu.VMEM((NX, NZ * GROUP, FF), bf16),
+            pltpu.VMEM((2, 3 * GROUP, FF), f32),
+            pltpu.VMEM((NX, NZ * GROUP, 256), bf16),
+            pltpu.VMEM((NX, NZ * ROWS, 128), bf16),
+            pltpu.VMEM((3 * GROUP, 128), bf16),
             pltpu.VMEM((NZ * GROUP, SLICE), f32),
             pltpu.VMEM((2, 7, GROUP, HALF), bf16),
             pltpu.VMEM((2, 7, GROUP, HALF), bf16),
@@ -427,7 +506,7 @@
         cost_estimate=pl.CostEstimate(
             flops=2 * 512 * D * FF * 3, bytes_accessed=16 * 2**20, transcendentals=512 * FF
         ),
-    )(counts, live, lengths, rows, gate, up, down, queries, cache)
+    )(counts, live, lengths, rows, gate.T, up.T, down, queries, cache)
 
 
 def solution(mesh):

time: 140 us -> 99 us (0.71)
  Pallas kernels: 120 us -> 94.4 us
  local copies, waits for them, and re-layouts: 18.1 us -> 3.31 us
    pallas_call x1, Pallas kernels: 120 us -> 94.4 us  [body(): pl.pallas_call(kernel, out_shape=(jax.ShapeDtypeStruct((ROWS, D), bf16),...]
    unnamed x4 -> x2, local copies, waits for them, and re-layouts: 18.1 us -> 3.31 us
where the time goes in v2:
time: 99 us; the launch traced here: 98.4 us
  Pallas kernels  94.4 us (95%)
  local copies, waits for them, and re-layouts  3.31 us (3%)
    pallas_call x1, Pallas kernels, body(): pl.pallas_call(kernel, out_shape=(jax.ShapeDtypeStruct((ROWS, D), bf16),...  94.4 us
    unnamed x2, local copies, waits for them, and re-layouts  3.31 us

profile of v2, /device:TPU:16, one launch (start us, length us, event | category | flops | bytes accessed | tf_op | source)
XLA Modules:
  0.0 98.4 jit_solution(11110722283625120504)
XLA Ops:
  0.6 94.4 %shard_map.104 = (bf16[16,7168]{1,0:T(8,128)(2,1)}, bf16[4,64,512]{2,1,0:T(8,128)(2,1)}) custom-call(s32[32]{0:T(128)} %counts.1, s32[32]{0:T(128)} %live.1, s32[128]{0:T(128)} %lengths.1, bf16[16,7168]{1,0:T(8,128)(2,1)} %rows_in.1, bf16[288,7168]{1,0:T(8,128)(2,1)} %bitcast.2, bf16[288,7168]{1,0:T(8,128)(2,1)} %bitcast.3, bf16[288,7168]{1,0:T(8,128)(2,1)} %wd_in.1, ...), custom_call_target="tpu_custom_call" | custom-call | flops 6341787648 | bytes 16777216 | tf_op jit(solution)/shard_map/pallas_call | solution.py:475
  95.1 1.6 %copy.13 = bf16[16,7168]{1,0:T(8,128)(2,1)} copy(bf16[16,7168]{1,0:T(8,128)(2,1)} %get-tuple-element.4) | data formatting | bytes 458752
  96.7 1.7 %copy.14 = bf16[4,64,512]{2,1,0:T(8,128)(2,1)} copy(bf16[4,64,512]{2,1,0:T(8,128)(2,1)} %get-tuple-element.5) | data formatting | bytes 524288

commit v3 on v2

--- a/solution.py
+++ b/solution.py
@@ -18,7 +18,7 @@
 A0 = 15 * TILE
 CB = D - CA
 B0 = 13 * TILE
-KCH = 1024
+KCH = 1792
 SUBS, SUB = 4, 16
 score_scale = 192.0 ** (-0.5)
 
@@ -41,7 +41,8 @@
     add("h", 24)
     add("ht", 24)
     add("r", 56)
-    add("f", 6)
+    add("f", 8)
+    add("n", 3)
     return names, len_box[0]
 
 
@@ -50,7 +51,7 @@
 
 def kernel(
     counts, live, lengths, rows_in, wg_in, wu_in, wd_in, q_in, c_in, ffn_out, attn_out,
-    xi, xb, wgu, wd, qb, cb, acc, hid, tail, rest, part, sbuf, rbuf, fs, fo, ssem, rsem, lsem,
+    xi, xb, wgu, wgt, wd, qb, cb, acc, hid, tail, rest, part, sbuf, rbuf, near, own, fin, ssem, rsem, lsem,
 ):
     inst = lax.axis_index("inst")
     rank = lax.axis_index("rank")
@@ -70,12 +71,18 @@
     other = (y * 2 + (1 - c), rank)
     zp, zm, xp, xm = at_z(1), at_z(-1), at_x(1), at_x(-1)
 
+    def beside(way, k):
+        return (inst, ((x + k) % NX) * NZ + (z + NZ + (1 if way == 0 else -1)) % NZ)
+
+
     loads = [
         pltpu.make_async_copy(rows_in, xi, lsem.at[0]),
         pltpu.make_async_copy(q_in, qb, lsem.at[1]),
         pltpu.make_async_copy(c_in, cb, lsem.at[2]),
-        pltpu.make_async_copy(wg_in, wgu.at[0:FF, :], lsem.at[3]),
-        pltpu.make_async_copy(wu_in, wgu.at[FF:2 * FF, :], lsem.at[4]),
+        pltpu.make_async_copy(wg_in.at[0:256, :], wgu.at[0:256, :], lsem.at[3]),
+        pltpu.make_async_copy(wu_in.at[0:256, :], wgu.at[256:512, :], lsem.at[4]),
+        pltpu.make_async_copy(wg_in.at[256:288, :], wgu.at[512:544, :], lsem.at[6]),
+        pltpu.make_async_copy(wu_in.at[256:288, :], wgu.at[544:576, :], lsem.at[7]),
         pltpu.make_async_copy(
             wd_in.at[:, pl.ds(pl.multiple_of(x * SLICE, TILE), SLICE)],
             wd.at[pl.ds(pl.multiple_of(x * FF, 16), FF), :],
@@ -86,6 +93,7 @@
 
     barrier = pltpu.get_barrier_semaphore()
     peers = [zp, zm, xp, xm, at_x(2), at_y(1), at_y(-1), at_y(2), other]
+    peers += [beside(way, k) for way in range(2) for k in (1, 2, 3)]
     for peer in peers:
         pl.semaphore_signal(barrier, inc=1, device_id=peer, device_id_type=MESH)
     for load in loads[1:]:
@@ -156,6 +164,8 @@
         ref = xb.at[block(0, dz), full_b]
         send(ref, ref, b2_index(dz, 0), xp)
         send(ref, ref, b2_index(dz, 1), xm)
+        if dz == 4:
+            send(ref, ref, b2_index(dz, 2), at_x(2))
 
     def b2_pass(dz):
         recv(xb.at[block(-1, dz), full_b], b2_index(dz, 0))
@@ -164,6 +174,10 @@
         recv(xb.at[block(1, dz), full_b], b2_index(dz, 1))
         ref = xb.at[block(1, dz), half_b[1]]
         send(ref, ref, b2_index(dz, 3), xm)
+
+    def b2_far():
+        for k, kind in ((1, 0), (3, 1), (2, 2)):
+            recv(xb.at[block(-k, 4), full_b], b2_index(4, kind))
 
     def b2_last(dz):
         recv(xb.at[block(-2, dz), half_b[0]], b2_index(dz, 2))
@@ -226,19 +240,19 @@
         keep = jnp.full((1, 1), slot, jnp.int32) < live[rank]
         attn_out[slot] = jnp.where(keep, value, 0.0).astype(jnp.bfloat16)
 
+    def turn_piece(k):
+        cols = pl.ds(k * 512, 512)
+        wgt[cols, :] = wgu[:, cols].T
+
     def up_piece(pair, k):
         cols = pl.ds(k * KCH, KCH)
         rows = jnp.concatenate([xb[group(dz), cols] for dz in pair], axis=0)
-        for which in range(2):
-            term = lax.dot_general(
-                rows, wgu[which * FF:(which + 1) * FF, cols], (((1,), (1,)), ((), ())),
-                preferred_element_type=jnp.float32,
-            )
-            size = len(pair) * GROUP
-            if k == 0:
-                acc[which, :size] = term
-            else:
-                acc[which, :size] += term
+        term = jnp.dot(rows, wgt[cols, :], preferred_element_type=jnp.float32)
+        size = len(pair) * GROUP
+        if k == 0:
+            acc[:size] = term
+        else:
+            acc[:size] += term
 
     def h_send(dz, part_of):
         for k in (1, 3, 2):
@@ -255,13 +269,17 @@
 
     def hidden_piece(pair):
         size = len(pair) * GROUP
-        gate, up = acc[0, :size], acc[1, :size]
-        value = (gate / (1.0 + jnp.exp(-gate)) * up).astype(jnp.bfloat16)
+
+        def gated(gate, up):
+            return (gate / (1.0 + jnp.exp(-gate)) * up).astype(jnp.bfloat16)
+
+        value = gated(acc[:size, 0:256], acc[:size, 256:512])
+        last_units = gated(acc[:size, 512:544], acc[:size, 544:576])
         for i, dz in enumerate(pair):
-            rows = value[i * GROUP:(i + 1) * GROUP]
-            hid[x, group(dz), :] = rows[:, :256]
+            hid[x, group(dz), :] = value[i * GROUP:(i + 1) * GROUP]
+            rows = last_units[i * GROUP:(i + 1) * GROUP]
             tail[x, quarter(dz), :] = jnp.concatenate(
-                [rows[n * ROWS:(n + 1) * ROWS, 256:] for n in range(4)], axis=1
+                [rows[n * ROWS:(n + 1) * ROWS] for n in range(4)], axis=1
             )
             h_send(dz, 0)
             h_send(dz, 1)
@@ -309,17 +327,30 @@
 
     def ring_step(step):
         for sub in range(SUBS):
-            rows = pl.ds(sub * SUB, SUB)
+            k = sub
+            to = (x + k) % NX
+            rows = pl.ds(pl.multiple_of(to * ROWS, ROWS), ROWS)
             for way in range(2):
                 index = SEM["r"] + (way * 7 + step) * SUBS + sub
                 dz = (-1 if way == 0 else 1) * (1 + step)
-                at = ((z + NZ + dz) % NZ) * GROUP + sub * SUB
-                value = part[pl.ds(pl.multiple_of(at, SUB), SUB), half_cols[way]]
+                value = part[block(k, dz), half_cols[way]]
                 if step > 0:
                     recv(rbuf.at[way, step - 1, rows], index - SUBS)
                     value = value + rbuf[way, step - 1, rows].astype(jnp.float32)
                 sbuf[way, step, rows] = value.astype(jnp.bfloat16)
-                send(sbuf.at[way, step, rows], rbuf.at[way, step, rows], index, toward[way])
+                if step < 6:
+                    send(sbuf.at[way, step, rows], rbuf.at[way, step, rows], index, toward[way])
+                else:
+                    send(sbuf.at[way, step, rows], fin.at[way, x], SEM["f"] + way * 4 + k, beside(way, k))
+
+    def near_send():
+        for k in range(4):
+            value = part[block(k, 0), :].astype(jnp.bfloat16)
+            if k == 0:
+                near[x] = value
+            else:
+                own[k] = value
+                send(own.at[k], near.at[x], SEM["n"] + k - 1, at_x(k))
 
     ways = ((0, -1), (1, 1))
 
@@ -363,23 +394,30 @@
     a1(2)
     for k in (1, 3, 2):
         w1_send(k)
+    for load in loads[3:]:
+        load.wait()
+    for k in range(D // 512):
+        pieces.append(functools.partial(turn_piece, k))
     a2(1, 0)
+    tick(2)
     b2_pass(0)
     attend(1)
     a2(1, 1)
-    attend(2)
+    tick(3)
     a2(1, 3)
+    tick(3)
     b2_pass(-1)
-    attend(3)
     a2(1, 2)
+    tick(3)
     b2_pass(1)
-    for load in loads[3:]:
-        load.wait()
-
+    drain()
     b1(2)
     a2(2, 0)
+    tick(4)
+    attend(2)
     last(0)
     a2(2, 1)
+    drain()
     last(1)
     queue_up((-1, 0, 1))
     tick(2)
@@ -395,6 +433,7 @@
     b1(3)
     drain()
     a2(3, 0)
+    attend(3)
     a2(3, 1)
     last(2)
     queue_up((-2, 2))
@@ -422,49 +461,39 @@
     a2(4, 0)
     last(3)
     queue_up((-3, 3))
-    tick(4)
+    drain()
     a2(4, 1)
-    b2_pass(4)
-    drain()
     queue_down((-2, 2))
     drain()
     ring_step(1)
     a2(4, 3)
     a2(4, 2)
-    for k in range(3):
+    for k in range(CA // KCH):
         up_piece((4,), k)
-    last(4)
-    for k in range(3, D // KCH):
+    b2_far()
+    for k in range(CA // KCH, D // KCH):
         up_piece((4,), k)
     hidden_piece((4,))
+    near_send()
     queue_down((-3, 3))
     drain()
     ring_step(2)
     queue_down((4,))
     drain()
-    for step in range(3, 7):
+    for step in range(3, 6):
         ring_step(step)
-
-    for way in range(2):
-        for sub in range(SUBS):
-            recv(rbuf.at[way, 6, pl.ds(sub * SUB, SUB)], SEM["r"] + (way * 7 + 6) * SUBS + sub)
-        value = part[group(0), half_cols[way]] + rbuf[way, 6].astype(jnp.float32)
-        fs[way] = value.astype(jnp.bfloat16)
-        cols = pl.ds(pl.multiple_of(x * SLICE + way * HALF, TILE), HALF)
-        for k in (1, 3, 2):
-            to = (x + k) % NX
-            send(
-                fs.at[way, pl.ds(pl.multiple_of(to * ROWS, ROWS), ROWS), :],
-                fo.at[:, cols], SEM["f"] + way * 3 + k - 1, at_x(k),
-            )
-        fo[:, cols] = fs[way, pl.ds(pl.multiple_of(x * ROWS, ROWS), ROWS), :]
+    ring_step(6)
     for copy in sent:
         copy.wait_send()
+    for k in (1, 2, 3):
+        recv(near.at[(x + NX - k) % NX], SEM["n"] + k - 1)
     for way in range(2):
-        for k in (1, 3, 2):
-            cols = pl.ds(pl.multiple_of(((x + NX - k) % NX) * SLICE + way * HALF, TILE), HALF)
-            recv(fo.at[:, cols], SEM["f"] + way * 3 + k - 1)
-    ffn_out[...] = fo[...]
+        for k in range(4):
+            recv(fin.at[way, (x + NX - k) % NX], SEM["f"] + way * 4 + k)
+    for xs in range(NX):
+        for way in range(2):
+            value = near[xs, :, half_cols[way]].astype(jnp.float32) + fin[way, xs].astype(jnp.float32)
+            ffn_out[:, xs * SLICE + way * HALF:xs * SLICE + (way + 1) * HALF] = value.astype(jnp.bfloat16)
 
 
 def body(rows, counts, gate, up, down, queries, cache, live, lengths):
@@ -484,21 +513,23 @@
             pltpu.VMEM((ROWS, D), bf16),
             pltpu.VMEM((NZ * GROUP, D), bf16),
             pltpu.VMEM((2 * FF, D), bf16),
+            pltpu.VMEM((D, 2 * FF), bf16),
             pltpu.VMEM((NX * FF, SLICE), bf16),
             pltpu.VMEM((4, 64, 576), bf16),
             pltpu.VMEM((4, 64, 576), bf16),
-            pltpu.VMEM((2, 3 * GROUP, FF), f32),
+            pltpu.VMEM((3 * GROUP, 2 * FF), f32),
             pltpu.VMEM((NX, NZ * GROUP, 256), bf16),
             pltpu.VMEM((NX, NZ * ROWS, 128), bf16),
             pltpu.VMEM((3 * GROUP, 128), bf16),
             pltpu.VMEM((NZ * GROUP, SLICE), f32),
             pltpu.VMEM((2, 7, GROUP, HALF), bf16),
-            pltpu.VMEM((2, 7, GROUP, HALF), bf16),
-            pltpu.VMEM((2, GROUP, HALF), bf16),
-            pltpu.VMEM((ROWS, D), bf16),
+            pltpu.VMEM((2, 6, GROUP, HALF), bf16),
+            pltpu.VMEM((NX, ROWS, SLICE), bf16),
+            pltpu.VMEM((NX, ROWS, SLICE), bf16),
+            pltpu.VMEM((2, NX, ROWS, HALF), bf16),
             pltpu.SemaphoreType.DMA((NSEM,)),
             pltpu.SemaphoreType.DMA((NSEM,)),
-            pltpu.SemaphoreType.DMA((6,)),
+            pltpu.SemaphoreType.DMA((8,)),
         ],
         compiler_params=pltpu.CompilerParams(
             collective_id=1, has_side_effects=True, vmem_limit_bytes=56 * 2**20

time: 99 us -> 94.6 us (0.956)
  Pallas kernels: 94.4 us -> 90.5 us
    pallas_call x1, Pallas kernels: 94.4 us -> 90.5 us  [body(): pl.pallas_call(kernel, out_shape=(jax.ShapeDtypeStruct((ROWS, D), bf16),...]
where the time goes in v3:
time: 94.6 us; the launch traced here: 94.4 us
  Pallas kernels  90.5 us (96%)
  local copies, waits for them, and re-layouts  3.31 us (3%)
    pallas_call x1, Pallas kernels, body(): pl.pallas_call(kernel, out_shape=(jax.ShapeDtypeStruct((ROWS, D), bf16),...  90.5 us
    unnamed x2, local copies, waits for them, and re-layouts  3.31 us

profile of v3, /device:TPU:16, one launch (start us, length us, event | category | flops | bytes accessed | tf_op | source)
XLA Modules:
  0.0 94.4 jit_solution(10115247087249499015)
XLA Ops:
  0.6 90.5 %shard_map.104 = (bf16[16,7168]{1,0:T(8,128)(2,1)}, bf16[4,64,512]{2,1,0:T(8,128)(2,1)}) custom-call(s32[32]{0:T(128)} %counts.1, s32[32]{0:T(128)} %live.1, s32[128]{0:T(128)} %lengths.1, bf16[16,7168]{1,0:T(8,128)(2,1)} %rows_in.1, bf16[288,7168]{1,0:T(8,128)(2,1)} %bitcast.2, bf16[288,7168]{1,0:T(8,128)(2,1)} %bitcast.3, bf16[288,7168]{1,0:T(8,128)(2,1)} %wd_in.1, ...), custom_call_target="tpu_custom_call" | custom-call | flops 6341787648 | bytes 16777216 | tf_op jit(solution)/shard_map/pallas_call | solution.py:504
  91.1 1.6 %copy.13 = bf16[16,7168]{1,0:T(8,128)(2,1)} copy(bf16[16,7168]{1,0:T(8,128)(2,1)} %get-tuple-element.4) | data formatting | bytes 458752
  92.8 1.7 %copy.14 = bf16[4,64,512]{2,1,0:T(8,128)(2,1)} copy(bf16[4,64,512]{2,1,0:T(8,128)(2,1)} %get-tuple-element.5) | data formatting | bytes 524288

commit v4 on v3

--- a/solution.py
+++ b/solution.py
@@ -113,6 +113,10 @@
         copy.start()
         sent.append(copy)
 
+    def settle(count):
+        for _ in range(count):
+            sent.pop(0).wait_send()
+
     def recv(dst, index):
         pltpu.make_async_remote_copy(
             dst, dst, ssem.at[index], rsem.at[index], device_id=zp, device_id_type=MESH
@@ -255,7 +259,7 @@
             acc[:size] += term
 
     def h_send(dz, part_of):
-        for k in (1, 3, 2):
+        for k in (2, 1, 3):
             at = ((dz % NZ) * 3 + k - 1)
             if part_of == 0:
                 ref = hid.at[x, group(dz), :]
@@ -326,7 +330,7 @@
     half_cols = (pl.ds(0, HALF), pl.ds(HALF, HALF))
 
     def ring_step(step):
-        for sub in range(SUBS):
+        for sub in (2, 1, 3, 0):
             k = sub
             to = (x + k) % NX
             rows = pl.ds(pl.multiple_of(to * ROWS, ROWS), ROWS)
@@ -388,108 +392,106 @@
     loads[1].wait()
     loads[2].wait()
     attend(0)
+    attend(1)
+    for k in (1, 3, 2):
+        w1_send(k)
+    b1(1)
     a1(1)
     a1(3)
-    b1(1)
-    a1(2)
-    for k in (1, 3, 2):
-        w1_send(k)
+    tick(3)
+    b1(2)
     for load in loads[3:]:
         load.wait()
     for k in range(D // 512):
         pieces.append(functools.partial(turn_piece, k))
+    a1(2)
+    w1_pass(3)
+    b2_pass(0)
+    a2(1, 1)
+    drain()
     a2(1, 0)
-    tick(2)
-    b2_pass(0)
-    attend(1)
-    a2(1, 1)
-    tick(3)
-    a2(1, 3)
-    tick(3)
-    b2_pass(-1)
     a2(1, 2)
     tick(3)
+    tick(2)
+    attend(3)
+    b2_pass(-1)
     b2_pass(1)
-    drain()
-    b1(2)
+    b1(3)
+    tick(2)
+    a2(1, 3)
+    tick(2)
+    last(0)
+    b2_pass(2)
     a2(2, 0)
-    tick(4)
+    a2(2, 1)
+    tick(3)
     attend(2)
-    last(0)
-    a2(2, 1)
-    drain()
+    w1_pass(1)
+    a2(2, 2)
+    tick(2)
+    b2_pass(-2)
     last(1)
     queue_up((-1, 0, 1))
-    tick(2)
-    w1_pass(1)
+    drain()
+    b2_pass(-3)
     a2(2, 3)
-    tick(2)
-    b2_pass(-2)
-    w1_pass(3)
-    a2(2, 2)
-    tick(2)
-    b2_pass(2)
+    b2_pass(3)
     w1_pass(2)
-    b1(3)
-    drain()
-    a2(3, 0)
-    attend(3)
-    a2(3, 1)
     last(2)
-    queue_up((-2, 2))
-    tick(2)
     for m in (1, 3, 2):
         w2_pass(1, m)
-    a2(3, 3)
-    tick(2)
-    b2_pass(-3)
+    queue_up((-2, 2))
+    tick(2)
+    tick(2)
+    tick(2)
+    a2(3, 1)
     for m in (1, 3, 2):
         w2_pass(3, m)
-    a2(3, 2)
-    tick(2)
-    b2_pass(3)
+    b1(4)
+    a2(3, 3)
     for m in (1, 3, 2):
         w2_pass(2, m)
-    drain()
-    b1(4)
+    a2(3, 0)
     for k in (1, 2, 3):
         for m in range(4):
             wc_recv(k, m)
     queue_down((-1, 0, 1))
     drain()
+    last(3)
+    a2(3, 2)
     ring_step(0)
+    queue_up((-3, 3))
+    queue_down((-2, 2))
+    drain()
+    ring_step(1)
+    a2(4, 2)
+    a2(4, 1)
     a2(4, 0)
-    last(3)
-    queue_up((-3, 3))
-    drain()
-    a2(4, 1)
-    queue_down((-2, 2))
-    drain()
-    ring_step(1)
+    b2_far()
     a2(4, 3)
-    a2(4, 2)
     for k in range(CA // KCH):
         up_piece((4,), k)
-    b2_far()
+    drain()
+    queue_down((-3, 3))
     for k in range(CA // KCH, D // KCH):
         up_piece((4,), k)
     hidden_piece((4,))
+    drain()
+    ring_step(2)
     near_send()
-    queue_down((-3, 3))
-    drain()
-    ring_step(2)
+    drain()
     queue_down((4,))
     drain()
-    for step in range(3, 6):
+    for step in range(3, 7):
+        before = len(sent)
         ring_step(step)
-    ring_step(6)
-    for copy in sent:
-        copy.wait_send()
+        settle(before)
     for k in (1, 2, 3):
         recv(near.at[(x + NX - k) % NX], SEM["n"] + k - 1)
     for way in range(2):
         for k in range(4):
             recv(fin.at[way, (x + NX - k) % NX], SEM["f"] + way * 4 + k)
+    settle(len(sent))
     for xs in range(NX):
         for way in range(2):
             value = near[xs, :, half_cols[way]].astype(jnp.float32) + fin[way, xs].astype(jnp.float32)

time: 94.6 us -> 90.5 us (0.957)
  Pallas kernels: 90.5 us -> 86.4 us
    pallas_call x1, Pallas kernels: 90.5 us -> 86.4 us  [body(): pl.pallas_call(kernel, out_shape=(jax.ShapeDtypeStruct((ROWS, D), bf16),...]
where the time goes in v4:
time: 90.5 us; the launch traced here: 90.4 us
  Pallas kernels  86.4 us (95%)
  local copies, waits for them, and re-layouts  3.31 us (4%)
    pallas_call x1, Pallas kernels, body(): pl.pallas_call(kernel, out_shape=(jax.ShapeDtypeStruct((ROWS, D), bf16),...  86.4 us
    unnamed x2, local copies, waits for them, and re-layouts  3.31 us

profile of v4, /device:TPU:16, one launch (start us, length us, event | category | flops | bytes accessed | tf_op | source)
XLA Modules:
  0.0 90.4 jit_solution(3504382700880969970)
XLA Ops:
  0.6 86.4 %shard_map.104 = (bf16[16,7168]{1,0:T(8,128)(2,1)}, bf16[4,64,512]{2,1,0:T(8,128)(2,1)}) custom-call(s32[32]{0:T(128)} %counts.1, s32[32]{0:T(128)} %live.1, s32[128]{0:T(128)} %lengths.1, bf16[16,7168]{1,0:T(8,128)(2,1)} %rows_in.1, bf16[288,7168]{1,0:T(8,128)(2,1)} %bitcast.2, bf16[288,7168]{1,0:T(8,128)(2,1)} %bitcast.3, bf16[288,7168]{1,0:T(8,128)(2,1)} %wd_in.1, ...), custom_call_target="tpu_custom_call" | custom-call | flops 6341787648 | bytes 16777216 | tf_op jit(solution)/shard_map/pallas_call | solution.py:506
  87.1 1.6 %copy.13 = bf16[16,7168]{1,0:T(8,128)(2,1)} copy(bf16[16,7168]{1,0:T(8,128)(2,1)} %get-tuple-element.4) | data formatting | bytes 458752
  88.7 1.7 %copy.14 = bf16[4,64,512]{2,1,0:T(8,128)(2,1)} copy(bf16[4,64,512]{2,1,0:T(8,128)(2,1)} %get-tuple-element.5) | data formatting | bytes 524288
